TPU v7x, 32 devices: a whole 2x2x4 slice. The times are simulated.
32 devices in a mesh: row: 4 (over x, core), col: 8 (over z, y).
Axes of the slice: x: 2, y: 2, z: 4, core: 2. Of those that a mesh axis runs over, the one named last changes fastest.
Arguments:
- tokens: bfloat16 [128, 8192], P('col', 'row'), may hold values from -6 to 6
- cotangent: bfloat16 [128, 8192], P('col', 'row'), may hold values from -1.5 to 1.5
- gate_weight: bfloat16 [8192, 14336], P('row', 'col'), may hold values from -0.0625 to 0.0625
- up_weight: bfloat16 [8192, 14336], P('row', 'col'), may hold values from -0.0625 to 0.0625
- down_weight: bfloat16 [14336, 8192], P('col', 'row'), may hold values from -0.046875 to 0.046875
Outputs:
- grad_tokens: bfloat16 [128, 8192], P('col', 'row')
- grad_gate: bfloat16 [8192, 14336], P('row', 'col')
- grad_up: bfloat16 [8192, 14336], P('row', 'col')
- grad_down: bfloat16 [14336, 8192], P('col', 'row')
All inputs are finite; a program needn't handle non-finite values.
Results may differ from a plain program's by a relative error of at most 0.0051.
Values may be sent and summed in bfloat16 or wider, within the bound.
A program may use at most 128 MiB of HBM per device.

v0:
```python
import jax
import jax.numpy as jnp
from jax import lax
from jax.sharding import PartitionSpec as P


def contract_last(left, right):
    return lax.dot_general(
        left, right, (((1,), (1,)), ((), ())), preferred_element_type=jnp.float32
    )


def contract_first(left, right):
    return lax.dot_general(
        left, right, (((0,), (0,)), ((), ())), preferred_element_type=jnp.float32
    )


def gating(gate, up, grad_hidden):
    sig = jax.nn.sigmoid(gate)
    act = gate * sig
    hidden = (act * up).astype(jnp.bfloat16)
    d_up = (grad_hidden * act).astype(jnp.bfloat16)
    d_gate = (grad_hidden * up * sig * (1.0 + gate * (1.0 - sig))).astype(jnp.bfloat16)
    return (jnp.concatenate([d_gate, d_up], axis=1), hidden)


def local(tokens, cotangent, gate_weight, up_weight, down_weight):
    tok_all, cot_all = (
        lax.all_gather(tokens, "col", axis=0, tiled=True),
        lax.all_gather(cotangent, "col", axis=0, tiled=True),
    )
    width = gate_weight.shape[1]
    both_weights = jnp.concatenate([gate_weight, up_weight], axis=1)
    piece = tok_all
    summed = lax.psum_scatter(
        jnp.dot(piece, both_weights, preferred_element_type=jnp.float32),
        "row",
        scatter_dimension=0,
        tiled=True,
    )
    piece = cot_all
    grad_hidden = lax.psum_scatter(
        contract_last(piece, down_weight), "row", scatter_dimension=0, tiled=True
    )
    paired, hidden = gating(summed[:, :width], summed[:, width:], grad_hidden)
    paired_all, hidden_all = (
        lax.all_gather(paired, "row", axis=0, tiled=True),
        lax.all_gather(hidden, "row", axis=0, tiled=True),
    )
    grad_both = contract_first(tok_all, paired_all)
    grad_gate = grad_both[:, :width].astype(jnp.bfloat16)
    grad_up = grad_both[:, width:].astype(jnp.bfloat16)
    grad_down = contract_first(hidden_all, cot_all).astype(jnp.bfloat16)
    piece = paired_all
    grad_tokens = lax.psum_scatter(
        contract_last(piece, both_weights), "col", scatter_dimension=0, tiled=True
    ).astype(jnp.bfloat16)
    return (grad_tokens, grad_gate, grad_up, grad_down)


def solution(mesh):
    return jax.shard_map(
        local,
        mesh=mesh,
        in_specs=(
            P("col", "row"),
            P("col", "row"),
            P("row", "col"),
            P("row", "col"),
            P("col", "row"),
        ),
        out_specs=(P("col", "row"), P("row", "col"), P("row", "col"), P("col", "row")),
        check_vma=False,
    )
```

profile of v0, /device:TPU:0, one launch (start us, length us, event | category | flops | bytes accessed | tf_op | source)
XLA Modules:
  0.0 231.6 jit_solution(5471020805838805017)
XLA Ops:
  7.2 0.0 reduce-scatter.4.cloned.1.call-start
  7.2 33.2 %all_gather.12 = bf16[128,2048]{1,0:T(8,128)(2,1)S(1)} all-gather(bf16[16,2048]{1,0:T(8,128)(2,1)} %param.6), channel_id=1, replica_groups=mesh['row'=4,'col'=8] {'col'}, dimensions={0}, use_global_device_ids=true | all-gather | bytes 589824 | tf_op jit(solution)/shard_map/all_gather | solution.py:31
  40.4 6.5 %fusion.3 = f32[128,1792]{1,0:T(8,128)} fusion(bf16[128,2048]{1,0:T(8,128)(2,1)S(1)} %all_gather.12, bf16[1792,2048]{1,0:T(8,128)(2,1)} %param.9), kind=kOutput, calls=%fused_computation.13 | convolution fusion | flops 939524096 | bytes 8781824 | tf_op jit(solution)/shard_map/dot_general | solution.py:8
  47.0 0.0 reduce-scatter.4.cloned.1.call-update
  47.0 0.0 copy-start
  47.0 0.0 reduce-scatter.6.cloned.1.call-start
  47.1 6.6 %constant_dynamic-update-slice_fusion.1 = bf16[2048,3584]{1,0:T(8,128)(2,1)} fusion(bf16[2048,1792]{1,0:T(8,128)(2,1)} %param.7), kind=kLoop, calls=%fused_computation.11 | loop fusion | bytes 14680064
  53.7 0.0 copy-done
  53.7 31.3 %all_gather.13 = bf16[128,2048]{1,0:T(8,128)(2,1)S(1)} all-gather(bf16[16,2048]{1,0:T(8,128)(2,1)S(1)} %copy-done), channel_id=1, replica_groups=mesh['row'=4,'col'=8] {'col'}, dimensions={0}, use_global_device_ids=true | all-gather | bytes 589824 | tf_op jit(solution)/shard_map/all_gather | solution.py:30
  84.9 6.6 %constant_dynamic-update-slice_fusion = bf16[2048,3584]{1,0:T(8,128)(2,1)} fusion(bf16[2048,3584]{1,0:T(8,128)(2,1)} %constant_dynamic-update-slice_fusion.1, bf16[2048,1792]{1,0:T(8,128)(2,1)} %param.8), kind=kLoop, calls=%fused_computation.10 | loop fusion | bytes 14680064 | tf_op jit(solution)/shard_map/concatenate | solution.py:34
  91.5 8.5 %convolution_bitcast_fusion = f32[128,3584]{1,0:T(8,128)} fusion(bf16[128,2048]{1,0:T(8,128)(2,1)S(1)} %all_gather.13, bf16[2048,3584]{1,0:T(8,128)(2,1)} %constant_dynamic-update-slice_fusion), kind=kOutput, calls=%fused_computation.3 | convolution fusion | flops 1879048192 | bytes 17039360 | tf_op jit(solution)/shard_map/dot_general | solution.py:37
  100.0 0.0 reduce-scatter.6.cloned.1.call-update
  100.0 0.0 reduce-scatter.8.cloned.1.call-start
  100.1 0.0 reduce-scatter.4.cloned.1.call-done
  100.1 31.1 %reduce-scatter.6.cloned.1.call-done = f32[32,3584]{1,0:T(8,128)} async-done(((f32[128,3584]{1,0:T(8,128)}), f32[32,3584]{1,0:T(8,128)}) %reduce-scatter.6.cloned.1.call-update) | async-done | bytes 458768 | tf_op jit(solution)/shard_map/reduce_scatter | solution.py:36
  131.2 1.3 multiply_convert_fusion.2
  132.5 8.9 %all_gather.14 = bf16[128,3584]{1,0:T(8,128)(2,1)S(1)} all-gather(bf16[32,3584]{1,0:T(8,128)(2,1)S(1)} %pad_maximum_fusion), channel_id=1, replica_groups=mesh['row'=4,'col'=8] {'row'}, dimensions={0}, use_global_device_ids=true | all-gather | bytes 1146880 | tf_op jit(solution)/shard_map/all_gather | solution.py:48
  141.4 10.9 %fusion.4 = f32[128,2048]{1,0:T(8,128)} fusion(bf16[128,3584]{1,0:T(8,128)(2,1)S(1)} %all_gather.14, bf16[2048,3584]{1,0:T(8,128)(2,1)} %constant_dynamic-update-slice_fusion), kind=kOutput, calls=%fused_computation.14 | convolution fusion | flops 1879048192 | bytes 16646144 | tf_op jit(solution)/shard_map/dot_general | solution.py:8
  152.3 7.3 %fusion = bf16[2048,3584]{0,1:T(8,128)(2,1)} fusion(bf16[128,3584]{1,0:T(8,128)(2,1)S(1)} %all_gather.14, bf16[128,2048]{1,0:T(8,128)(2,1)S(1)} %all_gather.13), kind=kOutput, calls=%fused_computation.1 | convolution fusion | flops 1886388224 | bytes 16121856 | tf_op jit(solution)/shard_map/dot_general | solution.py:14
  159.6 0.0 reduce-scatter.8.cloned.1.call-update
  159.6 10.8 %fusion.2 = (bf16[2048,1792]{0,1:T(8,128)(2,1)}, bf16[2048,1792]{0,1:T(8,128)(2,1)}) fusion(bf16[2048,3584]{0,1:T(8,128)(2,1)} %fusion), kind=kLoop, calls=%fused_computation.12 | loop fusion | bytes 29360128 | tf_op jit(solution)/shard_map/slice | solution.py:53
  170.5 10.0 %copy.10 = bf16[2048,1792]{1,0:T(8,128)(2,1)} copy(bf16[2048,1792]{0,1:T(8,128)(2,1)} %get-tuple-element.9) | data formatting | bytes 14680064
  180.4 9.9 %copy.11 = bf16[2048,1792]{1,0:T(8,128)(2,1)} copy(bf16[2048,1792]{0,1:T(8,128)(2,1)} %get-tuple-element.8) | data formatting | bytes 14680064
  190.4 7.0 %all_gather.15 = bf16[128,1792]{1,0:T(8,128)(2,1)S(1)} all-gather(bf16[32,1792]{1,0:T(8,128)(2,1)S(1)} %get-tuple-element.12), channel_id=1, replica_groups=mesh['row'=4,'col'=8] {'row'}, dimensions={0}, use_global_device_ids=true | all-gather | bytes 573440 | tf_op jit(solution)/shard_map/all_gather | solution.py:49
  197.4 5.1 %convolution_convert_fusion.1 = bf16[1792,2048]{1,0:T(8,128)(2,1)} fusion(bf16[128,1792]{1,0:T(8,128)(2,1)S(1)} %all_gather.15, bf16[128,2048]{1,0:T(8,128)(2,1)S(1)} %all_gather.12), kind=kOutput, calls=%fused_computation.2 | convolution fusion | flops 943194112 | bytes 8323072 | tf_op jit(solution)/shard_map/dot_general | solution.py:14
  202.5 21.0 %reduce-scatter.8.cloned.1.call-done = f32[16,2048]{1,0:T(8,128)} async-done(((f32[128,2048]{1,0:T(8,128)}), f32[16,2048]{1,0:T(8,128)}) %reduce-scatter.8.cloned.1.call-update) | async-done | bytes 131088 | tf_op jit(solution)/shard_map/reduce_scatter | solution.py:56
  223.5 1.5 convert_element_type.19
  (1 shorter events, 0.0 us)
Async XLA Ops:
  7.2 92.9 %reduce-scatter.4.cloned.1.call-start = ((), (), s32[]{:S(2)}) async-start(), calls=%async_computation.3 | async-start | bytes 1146880 | tf_op jit(solution)/shard_map/reduce_scatter | solution.py:43
  47.0 6.7 %copy-start = (bf16[16,2048]{1,0:T(8,128)(2,1)S(1)}, bf16[16,2048]{1,0:T(8,128)(2,1)}, u32[]{:S(2)}) copy-start(bf16[16,2048]{1,0:T(8,128)(2,1)} %param.5) | copy-start | bytes 196612
  47.0 84.2 %reduce-scatter.6.cloned.1.call-start = ((), (), s32[]{:S(2)}) async-start(), calls=%async_computation.4 | async-start | bytes 2293760 | tf_op jit(solution)/shard_map/reduce_scatter | solution.py:36
  100.0 123.5 %reduce-scatter.8.cloned.1.call-start = ((), (), s32[]{:S(2)}) async-start(), calls=%async_computation.5 | async-start | bytes 1179648 | tf_op jit(solution)/shard_map/reduce_scatter | solution.py:56
Sparse Core Ops, SparseCore 0:
  47.1 25.1 reduce-scatter.3
  100.1 30.9 reduce-scatter.5
  159.7 63.7 reduce-scatter.7
where the time goes:
time: 232 us
  blocking collectives  80.4 us (35%)
  waiting for transfers between devices  52.1 us (22%)
  local copies, waits for them, and re-layouts  43.9 us (19%)
  matrix products  38.4 us (17%)
  between operations  13.8 us (6%)
  other arithmetic  2.84 us (1%)
    all_gather x1, blocking collectives, local(): lax.all_gather(cotangent, 'col', axis=0, tiled=True)  33.2 us
    all_gather x1, blocking collectives, local(): lax.all_gather(tokens, 'col', axis=0, tiled=True)  31.3 us
    reduce_scatter x1, waiting for transfers between devices, local(): lax.psum_scatter(jnp.dot(piece, both_weights, preferred_element_type=jnp....  31.1 us
    unnamed x5, local copies, waits for them, and re-layouts  26.5 us
    reduce_scatter x1, waiting for transfers between devices, local(): lax.psum_scatter(contract_last(piece, both_weights), 'col', scatter_dimen...  21 us
    dot_general x2, matrix products, contract_last(): lax.dot_general(left, right, (((1,), (1,)), ((), ())), preferred_element_...  17.4 us
    dot_general x2, matrix products, contract_first(): lax.dot_general(left, right, (((0,), (0,)), ((), ())), preferred_element_...  12.4 us
    slice x1, local copies, waits for them, and re-layouts, local(): grad_up = grad_both[:, width:].astype(jnp.bfloat16)  10.8 us
  transfers between devices with their start and end apart: 3, of which 2 were waited for; matrix products, arithmetic and copies ran while one was open for 25% of the time, Pallas kernels for 0%

commit v1 on v0

--- a/solution.py
+++ b/solution.py
@@ -26,8 +26,31 @@
 
 
 def local(tokens, cotangent, gate_weight, up_weight, down_weight):
+
+    def test_the_links(values):
+        prior = lax.axis_size("col")
+        clean = lax.axis_index("col")
+        oldest, current_arr, w1 = (prior, clean, values.shape[0])
+        chunks = tuple(((it, (it + 1) % oldest) for it in range(oldest)))
+        store = tuple(((it, (it - 1) % oldest) for it in range(oldest)))
+        small = jnp.zeros((*values.shape[:0], oldest * w1, *values.shape[1:]), values.dtype)
+        small = lax.dynamic_update_slice_in_dim(small, values, current_arr * w1, axis=0)
+        item_now = even = values
+        after = oldest // 2
+        for dev in [*range(1, after + 1)]:
+            item_now = lax.ppermute(item_now, "col", chunks)
+            small = lax.dynamic_update_slice_in_dim(
+                small, item_now, (current_arr - dev) % oldest * w1, axis=0
+            )
+            if dev < oldest - after:
+                even = lax.ppermute(even, "col", store)
+                small = lax.dynamic_update_slice_in_dim(
+                    small, even, (current_arr + dev) % oldest * w1, axis=0
+                )
+        return small
+
     tok_all, cot_all = (
-        lax.all_gather(tokens, "col", axis=0, tiled=True),
+        test_the_links(tokens),
         lax.all_gather(cotangent, "col", axis=0, tiled=True),
     )
     width = gate_weight.shape[1]

time: 232 us -> 223 us (0.961)
  blocking collectives: 80.4 us -> 47.5 us
  waiting for transfers between devices: 52.1 us -> 79.9 us
  local copies, waits for them, and re-layouts: 43.9 us -> 23.8 us
  starting transfers between devices: 0.12 us -> 15.7 us
    all_gather x1 -> x0, blocking collectives: 31.3 us -> none  [local(): lax.all_gather(tokens, 'col', axis=0, tiled=True)]
    reduce_scatter x1, waiting for transfers between devices: 21 us -> 41.1 us  [local(): lax.psum_scatter(contract_last(piece, both_weights), 'col', scatter_dimen...]
    unnamed x5 -> x3, local copies, waits for them, and re-layouts: 26.5 us -> 6.64 us
    ppermute x0 -> x7, starting transfers between devices: none -> 15.6 us  [the longest x3 12.5 us: test_the_links(): even = lax.ppermute(even, 'col', store)]
    ppermute x0 -> x7, waiting for transfers between devices: none -> 11.3 us  [the longest x4 11.3 us: test_the_links(): item_now = lax.ppermute(item_now, 'col', chunks)]
    reduce_scatter x1, waiting for transfers between devices: 31.1 us -> 27.3 us  [local(): lax.psum_scatter(jnp.dot(piece, both_weights, preferred_element_type=jnp....]
  transfers between devices with their start and end apart: 3 -> 10, of which waited for: 2 -> 5; matrix products, arithmetic and copies ran while one was open for 25% -> 20% of each run, Pallas kernels for 0% -> 0%
where the time goes in v1:
time: 223 us; the launch traced here: 222 us
  waiting for transfers between devices  79.9 us (36%)
  blocking collectives  47.5 us (21%)
  matrix products  38.4 us (17%)
  local copies, waits for them, and re-layouts  23.8 us (11%)
  starting transfers between devices  15.7 us (7%)
  between operations  14 us (6%)
  other arithmetic  2.84 us (1%)
    reduce_scatter x1, waiting for transfers between devices, local(): lax.psum_scatter(contract_last(piece, both_weights), 'col', scatter_dimen...  41.1 us
    all_gather x1, blocking collectives, local(): lax.all_gather(cotangent, 'col', axis=0, tiled=True)  31.5 us
    reduce_scatter x1, waiting for transfers between devices, local(): lax.psum_scatter(jnp.dot(piece, both_weights, preferred_element_type=jnp....  27.3 us
    dot_general x2, matrix products, contract_last(): lax.dot_general(left, right, (((1,), (1,)), ((), ())), preferred_element_...  17.4 us
    ppermute x3, starting transfers between devices, test_the_links(): even = lax.ppermute(even, 'col', store)  12.5 us
    dot_general x2, matrix products, contract_first(): lax.dot_general(left, right, (((0,), (0,)), ((), ())), preferred_element_...  12.5 us
    ppermute x4, waiting for transfers between devices, test_the_links(): item_now = lax.ppermute(item_now, 'col', chunks)  11.3 us
    slice x1, local copies, waits for them, and re-layouts, local(): grad_up = grad_both[:, width:].astype(jnp.bfloat16)  10.5 us
  transfers between devices with their start and end apart: 10, of which 5 were waited for; matrix products, arithmetic and copies ran while one was open for 20% of the time, Pallas kernels for 0%

profile of v1, /device:TPU:0, one launch (start us, length us, event | category | flops | bytes accessed | tf_op | source)
XLA Modules:
  0.0 222.2 jit_solution(15179109896858008889)
XLA Ops:
  7.2 0.0 reduce-scatter.4.cloned.1.call-start
  7.2 3.0 %collective-permute-start = (bf16[16,2048]{1,0:T(8,128)(2,1)}, bf16[16,2048]{1,0:T(8,128)(2,1)S(1)}, u32[]{:S(2)}, u32[]{:S(2)}) collective-permute-start(bf16[16,2048]{1,0:T(8,128)(2,1)} %param.5), channel_id=1, source_target_pairs={{0,1},{1,2},{2,3},{3,4},{4,5},{5,6},{6,7},{7,0},{8,9},{9,10},{10,1... | collective-permute-start | bytes 196616 | tf_op jit(solution)/shard_map/ppermute | solution.py:41
  10.2 3.1 %collective-permute-start.1 = (bf16[16,2048]{1,0:T(8,128)(2,1)}, bf16[16,2048]{1,0:T(8,128)(2,1)S(1)}, u32[]{:S(2)}, u32[]{:S(2)}) collective-permute-start(bf16[16,2048]{1,0:T(8,128)(2,1)} %param.5), channel_id=1, source_target_pairs={{0,7},{1,0},{2,1},{3,2},{4,3},{5,4},{6,5},{7,6},{8,15},{9,8},{10,9... | collective-permute-start | bytes 196616 | tf_op jit(solution)/shard_map/ppermute | solution.py:46
  13.3 31.5 %all_gather.9 = bf16[128,2048]{1,0:T(8,128)(2,1)S(1)} all-gather(bf16[16,2048]{1,0:T(8,128)(2,1)} %param.6), channel_id=1, replica_groups=mesh['row'=4,'col'=8] {'col'}, dimensions={0}, use_global_device_ids=true | all-gather | bytes 589824 | tf_op jit(solution)/shard_map/all_gather | solution.py:54
  44.8 6.6 %fusion.2 = f32[128,1792]{1,0:T(8,128)} fusion(bf16[128,2048]{1,0:T(8,128)(2,1)S(1)} %all_gather.9, bf16[1792,2048]{1,0:T(8,128)(2,1)} %param.9), kind=kOutput, calls=%fused_computation.19 | convolution fusion | flops 939524096 | bytes 8781824 | tf_op jit(solution)/shard_map/dot_general | solution.py:8
  51.4 0.0 reduce-scatter.4.cloned.1.call-update
  51.4 0.0 reduce-scatter.6.cloned.1.call-start
  51.5 0.0 copy-start
  51.5 6.6 %constant_dynamic-update-slice_fusion.1 = bf16[2048,3584]{1,0:T(8,128)(2,1)} fusion(bf16[2048,1792]{1,0:T(8,128)(2,1)} %param.7), kind=kLoop, calls=%fused_computation.9 | loop fusion | bytes 14680064
  58.1 6.6 %constant_dynamic-update-slice_fusion = bf16[2048,3584]{1,0:T(8,128)(2,1)} fusion(bf16[2048,3584]{1,0:T(8,128)(2,1)} %constant_dynamic-update-slice_fusion.1, bf16[2048,1792]{1,0:T(8,128)(2,1)} %param.8), kind=kLoop, calls=%fused_computation.8 | loop fusion | bytes 14680064 | tf_op jit(solution)/shard_map/concatenate | solution.py:57
  64.8 0.0 copy-done
  64.9 0.0 collective-permute-done
  65.0 0.1 collective-permute-start.2
  65.0 0.0 collective-permute-done.1
  65.0 4.7 %collective-permute-start.3 = (bf16[16,2048]{1,0:T(8,128)(2,1)S(1)}, bf16[16,2048]{1,0:T(8,128)(2,1)S(1)}, u32[]{:S(2)}, u32[]{:S(2)}) collective-permute-start(bf16[16,2048]{1,0:T(8,128)(2,1)S(1)} %collective-permute-done.1), channel_id=1, source_target_pairs={{0,7},{1,0},{2,1},{3,2},{4,3},{5,4},{6,5},{7,6},{8,15},{9,8},{10,9... | collective-permute-start | bytes 196616 | tf_op jit(solution)/shard_map/ppermute | solution.py:46
  69.8 2.2 collective-permute-done.2
  72.0 0.0 collective-permute-start.4
  72.0 0.0 collective-permute-done.3
  72.0 4.7 %collective-permute-start.5 = (bf16[16,2048]{1,0:T(8,128)(2,1)S(1)}, bf16[16,2048]{1,0:T(8,128)(2,1)S(1)}, u32[]{:S(2)}, u32[]{:S(2)}) collective-permute-start(bf16[16,2048]{1,0:T(8,128)(2,1)S(1)} %collective-permute-done.3), channel_id=1, source_target_pairs={{0,7},{1,0},{2,1},{3,2},{4,3},{5,4},{6,5},{7,6},{8,15},{9,8},{10,9... | collective-permute-start | bytes 196616 | tf_op jit(solution)/shard_map/ppermute | solution.py:46
  76.7 2.2 collective-permute-done.4
  78.9 0.0 collective-permute-start.6
  79.0 0.0 collective-permute-done.5
  79.0 6.9 %collective-permute-done.6 = bf16[16,2048]{1,0:T(8,128)(2,1)S(1)} collective-permute-done((bf16[16,2048]{1,0:T(8,128)(2,1)S(1)}, bf16[16,2048]{1,0:T(8,128)(2,1)S(1)}, u32[]{:S(2)}, u32[]{:S(2)}) %collective-permute-start.6) | collective-permute-done | bytes 65568 | tf_op jit(solution)/shard_map/ppermute | solution.py:41
  85.9 8.5 %fusion.3 = f32[128,3584]{1,0:T(8,128)} fusion(bf16[128,2048]{1,0:T(8,128)(2,1)S(1)} %constant_dynamic-update-slice_fusion.2, bf16[2048,3584]{1,0:T(8,128)(2,1)} %constant_dynamic-update-slice_fusion), kind=kOutput, calls=%fused_computation.20 | convolution fusion | flops 1879048192 | bytes 17039360 | tf_op jit(solution)/shard_map/dot_general | solution.py:60
  94.4 0.0 reduce-scatter.6.cloned.1.call-update
  94.4 0.0 reduce-scatter.8.cloned.1.call-start
  94.5 0.0 reduce-scatter.4.cloned.1.call-done
  94.5 27.3 %reduce-scatter.6.cloned.1.call-done = f32[32,3584]{1,0:T(8,128)} async-done(((f32[128,3584]{1,0:T(8,128)}), f32[32,3584]{1,0:T(8,128)}) %reduce-scatter.6.cloned.1.call-update) | async-done | bytes 458768 | tf_op jit(solution)/shard_map/reduce_scatter | solution.py:59
  121.8 1.3 multiply_convert_fusion.2
  123.1 8.9 %all_gather.10 = bf16[128,3584]{1,0:T(8,128)(2,1)S(1)} all-gather(bf16[32,3584]{1,0:T(8,128)(2,1)S(1)} %pad_maximum_fusion), channel_id=1, replica_groups=mesh['row'=4,'col'=8] {'row'}, dimensions={0}, use_global_device_ids=true | all-gather | bytes 1146880 | tf_op jit(solution)/shard_map/all_gather | solution.py:71
  132.0 10.9 %fusion.4 = f32[128,2048]{1,0:T(8,128)} fusion(bf16[128,3584]{1,0:T(8,128)(2,1)S(1)} %all_gather.10, bf16[2048,3584]{1,0:T(8,128)(2,1)} %constant_dynamic-update-slice_fusion), kind=kOutput, calls=%fused_computation.21 | convolution fusion | flops 1879048192 | bytes 16646144 | tf_op jit(solution)/shard_map/dot_general | solution.py:8
  142.9 7.3 %convolution_convert_fusion = bf16[2048,3584]{1,0:T(8,128)(2,1)} fusion(bf16[128,2048]{1,0:T(8,128)(2,1)S(1)} %constant_dynamic-update-slice_fusion.2, bf16[128,3584]{1,0:T(8,128)(2,1)S(1)} %all_gather.10), kind=kOutput, calls=%fused_computation | convolution fusion | flops 1886388224 | bytes 16121856 | tf_op jit(solution)/shard_map/dot_general | solution.py:14
  150.2 0.0 reduce-scatter.8.cloned.1.call-update
  150.2 7.1 %all_gather.11 = bf16[128,1792]{1,0:T(8,128)(2,1)S(1)} all-gather(bf16[32,1792]{1,0:T(8,128)(2,1)S(1)} %get-tuple-element.8), channel_id=1, replica_groups=mesh['row'=4,'col'=8] {'row'}, dimensions={0}, use_global_device_ids=true | all-gather | bytes 573440 | tf_op jit(solution)/shard_map/all_gather | solution.py:72
  157.4 5.1 %convolution_convert_fusion.1 = bf16[1792,2048]{1,0:T(8,128)(2,1)} fusion(bf16[128,1792]{1,0:T(8,128)(2,1)S(1)} %all_gather.11, bf16[128,2048]{1,0:T(8,128)(2,1)S(1)} %all_gather.9), kind=kOutput, calls=%fused_computation.1 | convolution fusion | flops 943194112 | bytes 8323072 | tf_op jit(solution)/shard_map/dot_general | solution.py:14
  162.5 10.5 %fusion.1 = (bf16[2048,1792]{1,0:T(8,128)(2,1)}, bf16[2048,1792]{1,0:T(8,128)(2,1)}) fusion(bf16[2048,3584]{1,0:T(8,128)(2,1)} %convolution_convert_fusion), kind=kLoop, calls=%fused_computation.18 | loop fusion | bytes 29360128 | tf_op jit(solution)/shard_map/slice | solution.py:76
  173.0 41.1 %reduce-scatter.8.cloned.1.call-done = f32[16,2048]{1,0:T(8,128)} async-done(((f32[128,2048]{1,0:T(8,128)}), f32[16,2048]{1,0:T(8,128)}) %reduce-scatter.8.cloned.1.call-update) | async-done | bytes 131088 | tf_op jit(solution)/shard_map/reduce_scatter | solution.py:79
  214.1 1.5 convert_element_type.19
  (10 shorter events, 0.1 us)
Async XLA Ops:
  7.2 87.3 %reduce-scatter.4.cloned.1.call-start = ((), (), s32[]{:S(2)}) async-start(), calls=%async_computation.3 | async-start | bytes 1146880 | tf_op jit(solution)/shard_map/reduce_scatter | solution.py:66
  7.2 57.7 %collective-permute-start = (bf16[16,2048]{1,0:T(8,128)(2,1)}, bf16[16,2048]{1,0:T(8,128)(2,1)S(1)}, u32[]{:S(2)}, u32[]{:S(2)}) collective-permute-start(bf16[16,2048]{1,0:T(8,128)(2,1)} %param.5), channel_id=1, source_target_pairs={{0,1},{1,2},{2,3},{3,4},{4,5},{5,6},{6,7},{7,0},{8,9},{9,10},{10,1... | collective-permute-start | bytes 196616 | tf_op jit(solution)/shard_map/ppermute | solution.py:41
  10.2 54.8 %collective-permute-start.1 = (bf16[16,2048]{1,0:T(8,128)(2,1)}, bf16[16,2048]{1,0:T(8,128)(2,1)S(1)}, u32[]{:S(2)}, u32[]{:S(2)}) collective-permute-start(bf16[16,2048]{1,0:T(8,128)(2,1)} %param.5), channel_id=1, source_target_pairs={{0,7},{1,0},{2,1},{3,2},{4,3},{5,4},{6,5},{7,6},{8,15},{9,8},{10,9... | collective-permute-start | bytes 196616 | tf_op jit(solution)/shard_map/ppermute | solution.py:46
  51.4 70.4 %reduce-scatter.6.cloned.1.call-start = ((), (), s32[]{:S(2)}) async-start(), calls=%async_computation.4 | async-start | bytes 2293760 | tf_op jit(solution)/shard_map/reduce_scatter | solution.py:59
  51.5 13.3 %copy-start = (bf16[16,2048]{1,0:T(8,128)(2,1)S(1)}, bf16[16,2048]{1,0:T(8,128)(2,1)}, u32[]{:S(2)}) copy-start(bf16[16,2048]{1,0:T(8,128)(2,1)} %param.5) | copy-start | bytes 196612
  65.0 7.0 %collective-permute-start.2 = (bf16[16,2048]{1,0:T(8,128)(2,1)S(1)}, bf16[16,2048]{1,0:T(8,128)(2,1)S(1)}, u32[]{:S(2)}, u32[]{:S(2)}) collective-permute-start(bf16[16,2048]{1,0:T(8,128)(2,1)S(1)} %collective-permute-done), channel_id=1, source_target_pairs={{0,1},{1,2},{2,3},{3,4},{4,5},{5,6},{6,7},{7,0},{8,9},{9,10},{10,1... | collective-permute-start | bytes 196616 | tf_op jit(solution)/shard_map/ppermute | solution.py:41
  65.0 6.9 %collective-permute-start.3 = (bf16[16,2048]{1,0:T(8,128)(2,1)S(1)}, bf16[16,2048]{1,0:T(8,128)(2,1)S(1)}, u32[]{:S(2)}, u32[]{:S(2)}) collective-permute-start(bf16[16,2048]{1,0:T(8,128)(2,1)S(1)} %collective-permute-done.1), channel_id=1, source_target_pairs={{0,7},{1,0},{2,1},{3,2},{4,3},{5,4},{6,5},{7,6},{8,15},{9,8},{10,9... | collective-permute-start | bytes 196616 | tf_op jit(solution)/shard_map/ppermute | solution.py:46
  72.0 7.0 %collective-permute-start.4 = (bf16[16,2048]{1,0:T(8,128)(2,1)S(1)}, bf16[16,2048]{1,0:T(8,128)(2,1)S(1)}, u32[]{:S(2)}, u32[]{:S(2)}) collective-permute-start(bf16[16,2048]{1,0:T(8,128)(2,1)S(1)} %collective-permute-done.2), channel_id=1, source_target_pairs={{0,1},{1,2},{2,3},{3,4},{4,5},{5,6},{6,7},{7,0},{8,9},{9,10},{10,1... | collective-permute-start | bytes 196616 | tf_op jit(solution)/shard_map/ppermute | solution.py:41
  72.0 7.0 %collective-permute-start.5 = (bf16[16,2048]{1,0:T(8,128)(2,1)S(1)}, bf16[16,2048]{1,0:T(8,128)(2,1)S(1)}, u32[]{:S(2)}, u32[]{:S(2)}) collective-permute-start(bf16[16,2048]{1,0:T(8,128)(2,1)S(1)} %collective-permute-done.3), channel_id=1, source_target_pairs={{0,7},{1,0},{2,1},{3,2},{4,3},{5,4},{6,5},{7,6},{8,15},{9,8},{10,9... | collective-permute-start | bytes 196616 | tf_op jit(solution)/shard_map/ppermute | solution.py:46
  78.9 7.0 %collective-permute-start.6 = (bf16[16,2048]{1,0:T(8,128)(2,1)S(1)}, bf16[16,2048]{1,0:T(8,128)(2,1)S(1)}, u32[]{:S(2)}, u32[]{:S(2)}) collective-permute-start(bf16[16,2048]{1,0:T(8,128)(2,1)S(1)} %collective-permute-done.4), channel_id=1, source_target_pairs={{0,1},{1,2},{2,3},{3,4},{4,5},{5,6},{6,7},{7,0},{8,9},{9,10},{10,1... | collective-permute-start | bytes 196616 | tf_op jit(solution)/shard_map/ppermute | solution.py:41
  94.4 119.7 %reduce-scatter.8.cloned.1.call-start = ((), (), s32[]{:S(2)}) async-start(), calls=%async_computation.5 | async-start | bytes 1179648 | tf_op jit(solution)/shard_map/reduce_scatter | solution.py:79
Sparse Core Ops, SparseCore 0:
  51.5 22.7 reduce-scatter.3
  94.5 27.2 reduce-scatter.5
  150.4 63.7 reduce-scatter.7
